TPU v7x, 32 devices: a whole 2x2x4 slice. The times are simulated.
32 devices in a mesh: groups: 2 (over x), tensor: 16 (over z, y, core).
Axes of the slice: x: 2, y: 2, z: 4, core: 2. Of those that a mesh axis runs over, the one named last changes fastest.
Arguments:
- layer_input: bfloat16 [64, 8192], P(('groups', 'tensor')), parts along dimension 0, may hold values from -6 to 6
- cotangent: bfloat16 [64, 8192], P(('groups', 'tensor')), parts along dimension 0, may hold values from -3 to 3
- gate_values: bfloat16 [64, 14336], P('groups', 'tensor'), parts along dimension 0, may hold values from -6 to 6
- up_values: bfloat16 [64, 14336], P('groups', 'tensor'), parts along dimension 0, may hold values from -6 to 6
- gate_weight: bfloat16 [16384, 14336], P('groups', 'tensor'), parts along dimension 0, may hold values from -0.0625 to 0.0625
- up_weight: bfloat16 [16384, 14336], P('groups', 'tensor'), parts along dimension 0, may hold values from -0.0625 to 0.0625
- down_weight: bfloat16 [28672, 8192], P(('groups', 'tensor')), parts along dimension 0, may hold values from -0.046875 to 0.046875
Outputs:
- input_grad: bfloat16 [64, 8192], P(('groups', 'tensor')), parts along dimension 0
- gate_grad: bfloat16 [16384, 14336], P('groups', 'tensor'), parts along dimension 0
- up_grad: bfloat16 [16384, 14336], P('groups', 'tensor'), parts along dimension 0
- down_grad: bfloat16 [28672, 8192], P(('groups', 'tensor')), parts along dimension 0
- factor: bfloat16 [16384, 8192], P(('groups', 'tensor')), parts along dimension 0
There are 2 independent parts, one for each index of `groups`. A program takes and returns all parts, laid end to end along the dimension named above; each array names one. Nothing has to cross between parts.
All inputs are finite; a program needn't handle non-finite values.
Results may differ from a plain program's by a relative error of at most 0.0049.
Values may be sent and summed in bfloat16 or wider, within the bound.
A program may use at most 192 MiB of HBM per device.

v0:
```python
import jax
import jax.numpy as jnp
from jax import lax
from jax.sharding import PartitionSpec as P


def weight_grads(layer_input, gate_delta, up_delta):
    piece = lax.all_gather(layer_input, "tensor", axis=0, tiled=True)
    first = lax.dot_general(
        piece, gate_delta, (((0,), (0,)), ((), ())), preferred_element_type=jnp.float32
    )
    second = lax.dot_general(
        piece, up_delta, (((0,), (0,)), ((), ())), preferred_element_type=jnp.float32
    )
    return (first.astype(jnp.bfloat16), second.astype(jnp.bfloat16))


def input_grads(gate_delta, up_delta, gate_weight, up_weight):
    total = lax.dot_general(
        gate_delta, gate_weight, (((1,), (1,)), ((), ())), preferred_element_type=jnp.float32
    )
    return lax.psum_scatter(
        total
        + lax.dot_general(
            up_delta, up_weight, (((1,), (1,)), ((), ())), preferred_element_type=jnp.float32
        ),
        "tensor",
        scatter_dimension=0,
        tiled=True,
    ).astype(jnp.bfloat16)


def per_device(layer_input, cotangent, gate_values, up_values, gate_weight, up_weight, down_weight):
    gathered = lax.all_gather(cotangent, "tensor", axis=0, tiled=True)
    gate_float = gate_values.astype(jnp.float32)
    up_float = up_values.astype(jnp.float32)
    sigma = jax.nn.sigmoid(gate_float)
    activated = gate_float * sigma
    hidden = (activated * up_float).astype(jnp.bfloat16)
    hidden_grad = lax.dot_general(
        gathered, down_weight, (((1,), (1,)), ((), ())), preferred_element_type=jnp.float32
    )
    gate_delta = (hidden_grad * up_float * sigma * (1.0 + gate_float * (1.0 - sigma))).astype(
        jnp.bfloat16
    )
    up_delta = (hidden_grad * activated).astype(jnp.bfloat16)
    gate_grad, up_grad = weight_grads(layer_input, gate_delta, up_delta)
    input_grad = input_grads(gate_delta, up_delta, gate_weight, up_weight)
    down_grad = lax.dot_general(
        hidden, gathered, (((0,), (0,)), ((), ())), preferred_element_type=jnp.float32
    ).astype(jnp.bfloat16)
    factor_rows = gathered.shape[1] // lax.axis_size("tensor")
    owned = lax.dynamic_slice_in_dim(
        gathered, lax.axis_index("tensor") * factor_rows, factor_rows, 1
    )
    gram = lax.dot_general(
        owned, gathered, (((0,), (0,)), ((), ())), preferred_element_type=jnp.float32
    )
    factor = (gram / gathered.shape[0]).astype(jnp.bfloat16)
    return (input_grad, gate_grad, up_grad, down_grad, factor)


def solution(mesh):
    return jax.shard_map(
        per_device,
        mesh=mesh,
        in_specs=(
            P(("groups", "tensor"), None),
            P(("groups", "tensor"), None),
            P("groups", "tensor"),
            P("groups", "tensor"),
            P("groups", "tensor"),
            P("groups", "tensor"),
            P(("groups", "tensor"), None),
        ),
        out_specs=(
            P(("groups", "tensor"), None),
            P("groups", "tensor"),
            P("groups", "tensor"),
            P(("groups", "tensor"), None),
            P(("groups", "tensor"), None),
        ),
        check_vma=False,
    )
```

profile of v0, /device:TPU:0, one launch (start us, length us, event | category | flops | bytes accessed | tf_op | source)
XLA Modules:
  0.0 213.0 jit_solution(8348086152201650989)
XLA Ops:
  0.6 0.0 copy-start.1
  0.6 0.0 copy-start
  0.7 24.9 %all-gather = bf16[16,2,8192]{2,1,0:T(2,128)(2,1)S(1)} all-gather(bf16[1,2,8192]{2,1,0:T(2,128)(2,1)} %bitcast.17), channel_id=1, replica_groups=mesh['groups'=2,'tensor'=16] {'tensor'}, dimensions={0}, use_global_device_ids=true | all-gather | bytes 557056 | tf_op jit(solution)/shard_map/all_gather | solution.py:34
  25.6 0.2 reshape.11
  25.8 5.8 %multiply_convert_fusion = bf16[512,8192]{1,0:T(8,128)(2,1)} fusion(bf16[32,8192]{1,0:T(8,128)(2,1)S(1)} %reshape.11, s32[]{:T(128)S(6)} %select_n.3), kind=kOutput, calls=%fused_computation | convolution fusion | flops 276824064 | bytes 8945668 | tf_op jit(solution)/shard_map/dot_general | solution.py:56
  31.6 0.0 copy-done.1
  31.6 0.0 copy-done
  31.6 9.6 %fusion.2 = (bf16[32,896]{1,0:T(8,128)(2,1)S(1)}, f32[32,896]{1,0:T(8,128)S(1)}) fusion(bf16[32,896]{1,0:T(8,128)(2,1)S(1)} %copy-done.1, bf16[32,896]{1,0:T(8,128)(2,1)S(1)} %copy-done, bf16[32,8192]{1,0:T(8,128)(2,1)S(1)} %reshape.11, bf16[896,8192]{1,0:T(8,128)(2,1)} %param.13), kind=kOutput, calls=%fused_computation.12 | convolution fusion | flops 470106112 | bytes 15491072 | tf_op jit(solution)/shard_map/dot_general | solution.py:40
  41.1 0.0 copy-start.3
  41.2 0.0 copy-start.2
  41.2 9.6 %fusion.12 = f32[32,8192]{1,0:T(8,128)S(1)} fusion(bf16[32,896]{1,0:T(8,128)(2,1)S(1)} %get-tuple-element.15, bf16[8192,896]{1,0:T(8,128)(2,1)} %param.11), kind=kOutput, calls=%fused_computation.23 | convolution fusion | flops 469762048 | bytes 15785984 | tf_op jit(solution)/shard_map/dot_general | solution.py:19
  50.8 9.6 %convolution_add_fusion = f32[32,8192]{1,0:T(8,128)S(1)} fusion(f32[32,8192]{1,0:T(8,128)S(1)} %fusion.12, bf16[8192,896]{1,0:T(8,128)(2,1)} %param.12, f32[32,896]{1,0:T(8,128)S(1)} %get-tuple-element.16, bf16[32,896]{1,0:T(8,128)(2,1)S(1)} %copy-done), kind=kOutput, calls=%fused_computation.4 | convolution fusion | flops 470224896 | bytes 16949248 | tf_op jit(solution)/shard_map/dot_general | solution.py:24
  60.4 69.6 %all-reduce.2 = bf16[32,8192]{1,0:T(8,128)(2,1)S(1)} all-reduce(f32[32,8192]{1,0:T(8,128)S(1)} %convolution_add_fusion), channel_id=2, replica_groups=mesh['groups'=2,'tensor'=16] {'tensor'}, use_global_device_ids=true, to_apply=%region_0.0.clone | all-reduce | flops 262144 | bytes 1572864
  130.0 0.0 copy-done.3
  130.0 0.6 dynamic-slice
  131.2 0.7 dynamic-slice_convert_fusion
  131.9 0.0 copy-done.2
  131.9 18.9 %all-gather.1 = bf16[16,2,8192]{2,1,0:T(2,128)(2,1)S(1)} all-gather(bf16[1,2,8192]{2,1,0:T(2,128)(2,1)S(1)} %bitcast.18), channel_id=1, replica_groups=mesh['groups'=2,'tensor'=16] {'tensor'}, dimensions={0}, use_global_device_ids=true | all-gather | bytes 557056 | tf_op jit(solution)/shard_map/all_gather | solution.py:8
  150.7 0.2 reshape.13
  150.9 7.6 %convert_bitcast_fusion.1 = bf16[8192,896]{0,1:T(8,128)(2,1)} fusion(bf16[32,896]{1,0:T(8,128)(2,1)S(1)} %get-tuple-element.15, bf16[32,8192]{1,0:T(8,128)(2,1)S(1)} %reshape.13), kind=kOutput, calls=%fused_computation.2 | convolution fusion | flops 477102080 | bytes 15261696 | tf_op jit(solution)/shard_map/dot_general | solution.py:9
  158.5 19.7 %copy.14 = bf16[8192,896]{1,0:T(8,128)(2,1)} copy(bf16[8192,896]{0,1:T(8,128)(2,1)} %convert_bitcast_fusion.1) | data formatting | bytes 29360128
  178.2 7.6 %convert_bitcast_fusion = bf16[8192,896]{0,1:T(8,128)(2,1)} fusion(bf16[32,8192]{1,0:T(8,128)(2,1)S(1)} %reshape.13, f32[32,896]{1,0:T(8,128)S(1)} %get-tuple-element.16, bf16[32,896]{1,0:T(8,128)(2,1)S(1)} %copy-done), kind=kOutput, calls=%fused_computation.1 | convolution fusion | flops 477302784 | bytes 15376384 | tf_op jit(solution)/shard_map/dot_general | solution.py:12
  185.8 19.7 %copy.15 = bf16[8192,896]{1,0:T(8,128)(2,1)} copy(bf16[8192,896]{0,1:T(8,128)(2,1)} %convert_bitcast_fusion) | data formatting | bytes 29360128
  205.5 7.6 %convolution_convert_fusion = bf16[896,8192]{1,0:T(8,128)(2,1)} fusion(bf16[32,8192]{1,0:T(8,128)(2,1)S(1)} %reshape.11, bf16[32,896]{1,0:T(8,128)(2,1)S(1)} %copy-done.1, bf16[32,896]{1,0:T(8,128)(2,1)S(1)} %copy-done), kind=kOutput, calls=%fused_computation.3 | convolution fusion | flops 477331456 | bytes 15319040 | tf_op jit(solution)/shard_map/dot_general | solution.py:49
Async XLA Ops:
  0.6 30.9 %copy-start.1 = (bf16[32,896]{1,0:T(8,128)(2,1)S(1)}, bf16[32,896]{1,0:T(8,128)(2,1)}, u32[]{:S(2)}) copy-start(bf16[32,896]{1,0:T(8,128)(2,1)} %param.10) | copy-start | bytes 172036
  0.6 30.9 %copy-start = (bf16[32,896]{1,0:T(8,128)(2,1)S(1)}, bf16[32,896]{1,0:T(8,128)(2,1)}, u32[]{:S(2)}) copy-start(bf16[32,896]{1,0:T(8,128)(2,1)} %param.9) | copy-start | bytes 172036
  41.1 88.8 %copy-start.3 = (u32[32]{0:T(128)S(1)}, u32[32]{0:T(128)}, u32[]{:S(2)}) copy-start(u32[32]{0:T(128)} %constant.19) | copy-start | bytes 388
  41.2 90.7 %copy-start.2 = (bf16[2,8192]{1,0:T(2,128)(2,1)S(1)}, bf16[2,8192]{1,0:T(2,128)(2,1)}, u32[]{:S(2)}) copy-start(bf16[2,8192]{1,0:T(2,128)(2,1)} %param.7) | copy-start | bytes 98308
where the time goes:
time: 214 us; the launch traced here: 213 us
  blocking collectives  113 us (53%)
  matrix products  57.3 us (27%)
  local copies, waits for them, and re-layouts  41 us (19%)
    unnamed x1, blocking collectives  69.6 us
    unnamed x13, local copies, waits for them, and re-layouts  40.4 us
    all_gather x1, blocking collectives, per_device(): gathered = lax.all_gather(cotangent, 'tensor', axis=0, tiled=True)  24.9 us
    all_gather x1, blocking collectives, weight_grads(): piece = lax.all_gather(layer_input, 'tensor', axis=0, tiled=True)  18.9 us
    dot_general x1, matrix products, input_grads(): lax.dot_general(up_delta, up_weight, (((1,), (1,)), ((), ())), preferred_...  9.6 us
    dot_general x1, matrix products, input_grads(): lax.dot_general(gate_delta, gate_weight, (((1,), (1,)), ((), ())), prefer...  9.58 us
    dot_general x1, matrix products, per_device(): lax.dot_general(gathered, down_weight, (((1,), (1,)), ((), ())), preferre...  9.57 us
    dot_general x1, matrix products, weight_grads(): lax.dot_general(piece, gate_delta, (((0,), (0,)), ((), ())), preferred_el...  7.58 us

commit v1 on v0

v1 whole, which is shorter than its diff:
```python
import functools

import jax
import jax.numpy as jnp
from jax import lax
from jax.experimental import pallas as pl
from jax.experimental.pallas import tpu as pltpu
from jax.sharding import PartitionSpec as P

MESH = pl.DeviceIdType.MESH
FOLD = 8
F32 = jnp.float32
BF16 = jnp.bfloat16


def exchange_kernel(
    n,
    cot_ref, inp_ref, gate_ref, up_ref, gw_hbm, uw_hbm, dw_hbm,
    cot_out, inp_out, hidden_out, gd_out, ud_out, owned_out, ig_out,
    cot_g, inp_g, gw, uw, dw, acc, stack, part, landed,
    w_sem, cot_send, cot_recv, inp_send, inp_recv, rs_send, rs_recv,
):
    me = lax.axis_index("tensor")
    blk, width = cot_ref.shape
    tokens = cot_out.shape[0]

    dw_copy = pltpu.make_async_copy(dw_hbm, dw, w_sem.at[0])
    gw_copy = pltpu.make_async_copy(gw_hbm, gw, w_sem.at[1])
    uw_copy = pltpu.make_async_copy(uw_hbm, uw, w_sem.at[2])
    dw_copy.start()
    gw_copy.start()
    uw_copy.start()

    def peer(k):
        return lax.rem(me + k, n)

    def rows(p):
        return pl.ds(pl.multiple_of(p * blk, blk), blk)

    barrier = pltpu.get_barrier_semaphore()

    @pl.loop(1, n)
    def _(k):
        pl.semaphore_signal(barrier, inc=1, device_id={"tensor": peer(k)}, device_id_type=MESH)

    pl.semaphore_wait(barrier, n - 1)

    def send(src, dst, send_sem, recv_sem, k):
        return pltpu.make_async_remote_copy(
            src_ref=src, dst_ref=dst.at[rows(me)],
            send_sem=send_sem.at[k], recv_sem=recv_sem.at[me],
            device_id={"tensor": peer(k)}, device_id_type=MESH,
        )

    def arrival(dst, send_sem, recv_sem, k):
        p = peer(k)
        return pltpu.make_async_remote_copy(
            src_ref=dst.at[rows(p)], dst_ref=dst.at[rows(p)],
            send_sem=send_sem.at[k], recv_sem=recv_sem.at[p],
            device_id={"tensor": p}, device_id_type=MESH,
        )

    @pl.loop(1, n)
    def _(k):
        send(cot_ref, cot_g, cot_send, cot_recv, k).start()

    @pl.loop(1, n)
    def _(k):
        send(inp_ref, inp_g, inp_send, inp_recv, k).start()

    cot_g[rows(me), :] = cot_ref[...]
    inp_g[rows(me), :] = inp_ref[...]

    size = tokens * FOLD
    first = lax.broadcasted_iota(jnp.int32, (size, size), 0)
    second = lax.broadcasted_iota(jnp.int32, (size, size), 1)

    def unfold(src, dst):
        pick = (second == (first % tokens) * FOLD + first // tokens).astype(BF16)
        wide = jnp.dot(pick, src[...], preferred_element_type=F32).astype(BF16)
        for c in range(FOLD):
            dst[:, c * width:(c + 1) * width] = wide[c * tokens:(c + 1) * tokens]

    gate = gate_ref[...].astype(F32)
    up = up_ref[...].astype(F32)
    sigma = 1.0 / (1.0 + jnp.exp(-gate))
    act = gate * sigma
    hidden_out[...] = (act * up).astype(BF16)

    @pl.loop(1, n)
    def _(k):
        arrival(cot_g, cot_send, cot_recv, k).wait_recv()

    unfold(cot_g, cot_out)
    if owned_out is not None:
        own = owned_out.shape[1]
        owned_out[...] = cot_out[:, pl.ds(pl.multiple_of(me * own, own), own)]

    dw_copy.wait()
    acc[...] = jnp.zeros_like(acc)

    @pl.loop(0, FOLD)
    def _(c):
        cols = pl.ds(pl.multiple_of(c * width, width), width)
        acc[...] += lax.dot_general(
            cot_out[:, cols], dw[:, cols], (((1,), (1,)), ((), ())), preferred_element_type=F32
        )

    hg = acc[...]
    gd_out[...] = (hg * up * sigma * (1.0 + gate * (1.0 - sigma))).astype(BF16)
    ud_out[...] = (hg * act).astype(BF16)

    gw_copy.wait()
    uw_copy.wait()

    @pl.loop(0, FOLD)
    def _(c):
        here = pl.ds(pl.multiple_of(c * width, width), width)
        total = lax.dot_general(
            gd_out[...], gw[here, :], (((1,), (1,)), ((), ())), preferred_element_type=F32
        ) + lax.dot_general(
            ud_out[...], uw[here, :], (((1,), (1,)), ((), ())), preferred_element_type=F32
        )
        stack[pl.ds(pl.multiple_of(c * tokens, tokens), tokens), :] = total.astype(BF16)

    back = (second == (first % FOLD) * tokens + first // FOLD).astype(BF16)
    part[...] = jnp.dot(back, stack[...], preferred_element_type=F32).astype(BF16)

    def reduce_send(k):
        return pltpu.make_async_remote_copy(
            src_ref=part.at[rows(peer(k))], dst_ref=landed.at[rows(me)],
            send_sem=rs_send.at[k], recv_sem=rs_recv.at[me],
            device_id={"tensor": peer(k)}, device_id_type=MESH,
        )

    @pl.loop(1, n)
    def _(k):
        reduce_send(k).start()

    @pl.loop(1, n)
    def _(k):
        arrival(inp_g, inp_send, inp_recv, k).wait_recv()

    unfold(inp_g, inp_out)

    landed[rows(me), :] = part[rows(me), :]

    @pl.loop(1, n)
    def _(k):
        arrival(landed, rs_send, rs_recv, k).wait_recv()

    def add(p, total):
        return total + landed[rows(p), :].astype(F32)

    ig_out[...] = lax.fori_loop(0, n, add, jnp.zeros((blk, width), F32)).astype(BF16)

    @pl.loop(1, n)
    def _(k):
        send(cot_ref, cot_g, cot_send, cot_recv, k).wait_send()
        send(inp_ref, inp_g, inp_send, inp_recv, k).wait_send()
        reduce_send(k).wait_send()


def grads_kernel(tokens, cot_ref, inp_ref, hidden_ref, gd_ref, ud_ref, owned_ref,
                 gg_out, ug_out, dg_out, fac_out):
    dims = (((0,), (0,)), ((), ()))
    x = inp_ref[...]
    y = cot_ref[...]
    gg_out[...] = lax.dot_general(x, gd_ref[...], dims, preferred_element_type=F32).astype(BF16)
    ug_out[...] = lax.dot_general(x, ud_ref[...], dims, preferred_element_type=F32).astype(BF16)
    dg_out[...] = lax.dot_general(hidden_ref[...], y, dims, preferred_element_type=F32).astype(BF16)
    gram = lax.dot_general(owned_ref[...], y, dims, preferred_element_type=F32)
    if tokens & (tokens - 1) == 0:
        gram = gram * (1.0 / tokens)
    else:
        gram = gram / tokens
    fac_out[...] = gram.astype(BF16)


def per_device(n, layer_input, cotangent, gate_values, up_values, gate_weight, up_weight, down_weight):
    local, d = cotangent.shape
    tokens, ff = gate_values.shape
    width = d // FOLD
    blk = local * FOLD
    own = d // n
    inside = own % 128 == 0
    vmem = pl.BlockSpec(memory_space=pltpu.VMEM)
    hbm = pl.BlockSpec(memory_space=pl.ANY)
    shape = jax.ShapeDtypeStruct
    outs = [
        shape((tokens, d), BF16), shape((tokens, d), BF16),
        shape((tokens, ff), BF16), shape((tokens, ff), BF16), shape((tokens, ff), BF16),
        shape((tokens, own), BF16), shape((blk, width), BF16),
    ]
    body = functools.partial(exchange_kernel, n)
    if not inside:
        del outs[5]

        def body(*refs):
            return exchange_kernel(n, *refs[:12], None, *refs[12:])

    gathered = pltpu.VMEM((tokens * FOLD, width), BF16)
    results = pl.pallas_call(
        body,
        out_shape=outs,
        in_specs=[vmem] * 4 + [hbm] * 3,
        out_specs=[vmem] * len(outs),
        scratch_shapes=[
            gathered, gathered,
            pltpu.VMEM((d, ff), BF16), pltpu.VMEM((d, ff), BF16), pltpu.VMEM((ff, d), BF16),
            pltpu.VMEM((tokens, ff), F32),
            gathered, gathered, gathered,
            pltpu.SemaphoreType.DMA((3,)),
        ] + [pltpu.SemaphoreType.DMA((n,))] * 6,
        compiler_params=pltpu.CompilerParams(
            collective_id=0, has_side_effects=True, vmem_limit_bytes=60 * 2**20
        ),
        cost_estimate=pl.CostEstimate(
            flops=6 * tokens * d * ff, bytes_accessed=6 * d * ff, transcendentals=tokens * ff
        ),
        name="exchange",
    )(
        cotangent.reshape(blk, width), layer_input.reshape(blk, width),
        gate_values, up_values, gate_weight, up_weight, down_weight,
    )
    cot, inp, hidden, gd, ud = results[:5]
    if inside:
        owned = results[5]
    else:
        owned = lax.dynamic_slice_in_dim(cot, lax.axis_index("tensor") * own, own, 1)
    input_grad = results[-1].reshape(local, d)

    tile = d // 16
    whole = lambda a: pl.BlockSpec(a.shape, lambda i: (0, 0))
    gate_grad, up_grad, down_grad, factor = pl.pallas_call(
        functools.partial(grads_kernel, tokens),
        grid=(d // tile,),
        out_shape=[
            shape((d, ff), BF16), shape((d, ff), BF16), shape((ff, d), BF16), shape((own, d), BF16),
        ],
        in_specs=[
            pl.BlockSpec((tokens, tile), lambda i: (0, i)),
            pl.BlockSpec((tokens, tile), lambda i: (0, i)),
            whole(hidden), whole(gd), whole(ud), whole(owned),
        ],
        out_specs=[
            pl.BlockSpec((tile, ff), lambda i: (i, 0)),
            pl.BlockSpec((tile, ff), lambda i: (i, 0)),
            pl.BlockSpec((ff, tile), lambda i: (0, i)),
            pl.BlockSpec((own, tile), lambda i: (0, i)),
        ],
        compiler_params=pltpu.CompilerParams(vmem_limit_bytes=48 * 2**20),
        cost_estimate=pl.CostEstimate(
            flops=6 * tokens * d * ff + 2 * tokens * d * own,
            bytes_accessed=6 * d * ff + 2 * d * own, transcendentals=0,
        ),
        name="grads",
    )(cot, inp, hidden, gd, ud, owned)
    return (input_grad, gate_grad, up_grad, down_grad, factor)


def solution(mesh):
    return jax.shard_map(
        functools.partial(per_device, mesh.shape["tensor"]),
        mesh=mesh,
        in_specs=(
            P(("groups", "tensor"), None),
            P(("groups", "tensor"), None),
            P("groups", "tensor"),
            P("groups", "tensor"),
            P("groups", "tensor"),
            P("groups", "tensor"),
            P(("groups", "tensor"), None),
        ),
        out_specs=(
            P(("groups", "tensor"), None),
            P("groups", "tensor"),
            P("groups", "tensor"),
            P(("groups", "tensor"), None),
            P(("groups", "tensor"), None),
        ),
        check_vma=False,
    )
```

time: 214 us -> 77.3 us (0.36)
  the two profiles are of different devices: /device:TPU:0 before, /device:TPU:31 now
where the time goes in v1:
time: 77.3 us; the launch traced here: 76.6 us
  Pallas kernels  66.5 us (86%)
  local copies, waits for them, and re-layouts  9.47 us (12%)
    pallas_call x1, Pallas kernels, per_device(): pl.pallas_call(body, out_shape=outs, in_specs=[vmem] * 4 + [hbm] * 3, out...  48.4 us
    pallas_call x1, Pallas kernels, per_device(): pl.pallas_call(functools.partial(grads_kernel, tokens), grid=(d // tile,)...  18.1 us
    unnamed x12, local copies, waits for them, and re-layouts  5.29 us

profile of v1, /device:TPU:31, one launch (start us, length us, event | category | flops | bytes accessed | tf_op | source)
XLA Modules:
  0.0 76.6 jit_solution(10545217322092154773)
XLA Ops:
  0.6 1.4 %reshape.20.inp_ref = bf16[16,1024]{1,0:T(8,128)(2,1)} reshape(bf16[2,8192]{1,0:T(2,128)(2,1)} %param.7) | data formatting | bytes 65536 | tf_op jit(solution)/shard_map/reshape | solution.py:223
  2.0 1.4 %reshape.19.cot_ref = bf16[16,1024]{1,0:T(8,128)(2,1)} reshape(bf16[2,8192]{1,0:T(2,128)(2,1)} %param.8) | data formatting | bytes 65536 | tf_op jit(solution)/shard_map/reshape | solution.py:223
  3.4 48.4 %exchange.1 = (bf16[32,8192]{1,0:T(8,128)(2,1)}, bf16[32,8192]{1,0:T(8,128)(2,1)}, bf16[32,896]{1,0:T(8,128)(2,1)}, bf16[32,896]{1,0:T(8,128)(2,1)}, bf16[32,896...) custom-call(bf16[16,1024]{1,0:T(8,128)(2,1)} %reshape.19.cot_ref, ...), custom_call_target="tpu_custom_call" | custom-call | flops 1409286144 | bytes 44040192 | tf_op jit(solution)/shard_map/exchange/pallas_call | solution.py:203
  51.9 1.4 %reshape.21 = bf16[2,8192]{1,0:T(2,128)(2,1)} reshape(bf16[16,1024]{1,0:T(8,128)(2,1)} %get-tuple-element.16) | data formatting | bytes 65536 | tf_op jit(solution)/shard_map/reshape | solution.py:231
  53.3 0.0 copy-start
  53.3 1.0 %copy-done = bf16[32,8192]{1,0:T(8,128)(2,1)S(1)} copy-done((bf16[32,8192]{1,0:T(8,128)(2,1)S(1)}, bf16[32,8192]{1,0:T(8,128)(2,1)}, u32[]{:S(2)}) %copy-start) | copy-done | bytes 524312
  54.3 0.0 copy-start.1
  54.3 1.0 %copy-done.1 = bf16[32,8192]{1,0:T(8,128)(2,1)S(1)} copy-done((bf16[32,8192]{1,0:T(8,128)(2,1)S(1)}, bf16[32,8192]{1,0:T(8,128)(2,1)}, u32[]{:S(2)}) %copy-start.1) | copy-done | bytes 524312
  55.3 0.0 copy-start.2
  55.3 0.8 %copy-done.2 = bf16[32,896]{1,0:T(8,128)(2,1)S(1)} copy-done((bf16[32,896]{1,0:T(8,128)(2,1)S(1)}, bf16[32,896]{1,0:T(8,128)(2,1)}, u32[]{:S(2)}) %copy-start.2) | copy-done | bytes 57368
  56.2 0.0 copy-start.3
  56.2 0.8 %copy-done.3 = bf16[32,896]{1,0:T(8,128)(2,1)S(1)} copy-done((bf16[32,896]{1,0:T(8,128)(2,1)S(1)}, bf16[32,896]{1,0:T(8,128)(2,1)}, u32[]{:S(2)}) %copy-start.3) | copy-done | bytes 57368
  57.0 0.0 copy-start.4
  57.0 0.8 %copy-done.4 = bf16[32,896]{1,0:T(8,128)(2,1)S(1)} copy-done((bf16[32,896]{1,0:T(8,128)(2,1)S(1)}, bf16[32,896]{1,0:T(8,128)(2,1)}, u32[]{:S(2)}) %copy-start.4) | copy-done | bytes 57368
  57.8 0.0 copy-start.5
  57.8 0.8 copy-done.5
  58.6 18.1 %grads.1 = (bf16[8192,896]{1,0:T(8,128)(2,1)}, bf16[8192,896]{1,0:T(8,128)(2,1)}, bf16[896,8192]{1,0:T(8,128)(2,1)}, bf16[512,8192]{1,0:T(8,128)(2,1)}) custom-call(bf16[32,8192]{1,0:T(8,128)(2,1)S(1)} %copy-done, bf16[32,8192]{1,0:T(8,128)(2,1)S(1)} %copy-done.1, bf16[32,896]{1,0:T(8,128)(2,1)S(1)} %copy-done.2, bf16[32,896]{1,0:T(8,128)(2,1)S(1)} %copy-done.3, ...), custom_call_target="tpu_custom_call" | custom-call | flops 1677721600 | bytes 52428800 | tf_op jit(solution)/shard_map/grads/pallas_call | solution.py:235
Async XLA Ops:
  53.3 1.0 %copy-start = (bf16[32,8192]{1,0:T(8,128)(2,1)S(1)}, bf16[32,8192]{1,0:T(8,128)(2,1)}, u32[]{:S(2)}) copy-start(bf16[32,8192]{1,0:T(8,128)(2,1)} %get-tuple-element.17.cot_ref) | copy-start | bytes 1572868
  54.3 1.0 %copy-start.1 = (bf16[32,8192]{1,0:T(8,128)(2,1)S(1)}, bf16[32,8192]{1,0:T(8,128)(2,1)}, u32[]{:S(2)}) copy-start(bf16[32,8192]{1,0:T(8,128)(2,1)} %get-tuple-element.18.inp_ref) | copy-start | bytes 1572868
  55.3 0.8 %copy-start.2 = (bf16[32,896]{1,0:T(8,128)(2,1)S(1)}, bf16[32,896]{1,0:T(8,128)(2,1)}, u32[]{:S(2)}) copy-start(bf16[32,896]{1,0:T(8,128)(2,1)} %get-tuple-element.19.hidden_ref) | copy-start | bytes 172036
  56.2 0.8 %copy-start.3 = (bf16[32,896]{1,0:T(8,128)(2,1)S(1)}, bf16[32,896]{1,0:T(8,128)(2,1)}, u32[]{:S(2)}) copy-start(bf16[32,896]{1,0:T(8,128)(2,1)} %get-tuple-element.20.gd_ref) | copy-start | bytes 172036
  57.0 0.8 %copy-start.4 = (bf16[32,896]{1,0:T(8,128)(2,1)S(1)}, bf16[32,896]{1,0:T(8,128)(2,1)}, u32[]{:S(2)}) copy-start(bf16[32,896]{1,0:T(8,128)(2,1)} %get-tuple-element.21.ud_ref) | copy-start | bytes 172036
  57.8 0.8 copy-start.5

commit v2 on v1

v2 whole, which is shorter than its diff:
```python
import functools

import jax
import jax.numpy as jnp
from jax import lax
from jax.experimental import pallas as pl
from jax.experimental.pallas import tpu as pltpu
from jax.sharding import PartitionSpec as P

MESH = pl.DeviceIdType.MESH
FOLD = 8
PIECES = 4
F32 = jnp.float32
BF16 = jnp.bfloat16


def exchange_kernel(
    n,
    cot_ref, inp_ref, gate_ref, up_ref, gw_hbm, uw_hbm, dw_hbm,
    cot_out, inp_out, hidden_out, gd_out, ud_out, owned_out, ig_out,
    cot_g, inp_g, gw, uw, dw, acc, fold, stack, part, pair, half, landed,
    w_sem, cot_send, cot_recv, inp_send, inp_recv, swap_send, swap_recv,
    pair_send, pair_recv, rs_send, rs_recv,
):
    me = lax.axis_index("tensor")
    local, d = cot_ref.shape
    tokens = cot_out.shape[0]
    width = d // FOLD
    blk = local * FOLD
    chips = n // 2
    side = chips * blk
    step = width // PIECES
    core = lax.rem(me, 2)
    chip = lax.div(me, 2)
    twin = me + 1 - 2 * core

    dw_copy = pltpu.make_async_copy(dw_hbm, dw, w_sem.at[0])
    gw_copy = pltpu.make_async_copy(gw_hbm, gw, w_sem.at[1])
    uw_copy = pltpu.make_async_copy(uw_hbm, uw, w_sem.at[2])
    dw_copy.start()
    gw_copy.start()
    uw_copy.start()

    def there(k):
        return lax.rem(chip + k, chips)

    def device(c):
        return {"tensor": 2 * c + core}

    barrier = pltpu.get_barrier_semaphore()

    @pl.loop(1, chips)
    def _(k):
        pl.semaphore_signal(barrier, inc=1, device_id=device(there(k)), device_id_type=MESH)

    pl.semaphore_signal(barrier, inc=1, device_id={"tensor": twin}, device_id_type=MESH)

    def slot(c):
        return pl.ds(pl.multiple_of(core * side + c * blk, blk), blk)

    def block(c):
        return pl.ds(pl.multiple_of(c * blk, blk), blk)

    mine = pl.ds(pl.multiple_of(core * side, side), side)
    others = pl.ds(pl.multiple_of((1 - core) * side, side), side)

    def place(src, dst):
        x = src[...].astype(F32)
        for c in range(FOLD):
            fold[c * local:(c + 1) * local, :] = x[:, c * width:(c + 1) * width]
        dst[slot(chip), :] = fold[...].astype(BF16)

    def send(buf, send_sem, recv_sem, k):
        return pltpu.make_async_remote_copy(
            src_ref=buf.at[slot(chip)], dst_ref=buf.at[slot(chip)],
            send_sem=send_sem.at[k], recv_sem=recv_sem.at[chip],
            device_id=device(there(k)), device_id_type=MESH,
        )

    def arrival(buf, send_sem, recv_sem, k):
        c = there(k)
        return pltpu.make_async_remote_copy(
            src_ref=buf.at[slot(c)], dst_ref=buf.at[slot(c)],
            send_sem=send_sem.at[k], recv_sem=recv_sem.at[c],
            device_id=device(c), device_id_type=MESH,
        )

    def swap(buf, i, rows):
        return pltpu.make_async_remote_copy(
            src_ref=buf.at[rows], dst_ref=buf.at[rows],
            send_sem=swap_send.at[i], recv_sem=swap_recv.at[i],
            device_id={"tensor": twin}, device_id_type=MESH,
        )

    place(cot_ref, cot_g)
    place(inp_ref, inp_g)
    pl.semaphore_wait(barrier, chips)

    @pl.loop(1, chips)
    def _(k):
        send(cot_g, cot_send, cot_recv, k).start()

    size = tokens * FOLD
    first = lax.broadcasted_iota(jnp.int32, (size, size), 0)
    second = lax.broadcasted_iota(jnp.int32, (size, size), 1)

    def gathered_row(stacked):
        c, t = stacked // tokens, stacked % tokens
        owner, r = t // local, t % local
        return (owner % 2) * side + (owner // 2) * blk + c * local + r

    def unfold(src, dst):
        pick = (second == gathered_row(first)).astype(BF16)
        wide = jnp.dot(pick, src[...], preferred_element_type=F32).astype(BF16)
        for c in range(FOLD):
            dst[:, c * width:(c + 1) * width] = wide[c * tokens:(c + 1) * tokens]

    gate = gate_ref[...].astype(F32)
    up = up_ref[...].astype(F32)
    sigma = 1.0 / (1.0 + jnp.exp(-gate))
    act = gate * sigma
    hidden_out[...] = (act * up).astype(BF16)

    @pl.loop(1, chips)
    def _(k):
        arrival(cot_g, cot_send, cot_recv, k).wait_recv()

    swap(cot_g, 0, mine).start()

    @pl.loop(1, chips)
    def _(k):
        send(inp_g, inp_send, inp_recv, k).start()

    swap(cot_g, 0, others).wait_recv()
    unfold(cot_g, cot_out)
    if owned_out is not None:
        own = owned_out.shape[1]
        owned_out[...] = cot_out[:, pl.ds(pl.multiple_of(me * own, own), own)]

    dw_copy.wait()
    acc[...] = jnp.zeros_like(acc)

    @pl.loop(0, FOLD)
    def _(c):
        cols = pl.ds(pl.multiple_of(c * width, width), width)
        acc[...] += lax.dot_general(
            cot_out[:, cols], dw[:, cols], (((1,), (1,)), ((), ())), preferred_element_type=F32
        )

    hg = acc[...]
    gd_out[...] = (hg * up * sigma * (1.0 + gate * (1.0 - sigma))).astype(BF16)
    ud_out[...] = (hg * act).astype(BF16)

    @pl.loop(1, chips)
    def _(k):
        arrival(inp_g, inp_send, inp_recv, k).wait_recv()

    swap(inp_g, 1, mine).start()
    gw_copy.wait()
    uw_copy.wait()
    back = (first == gathered_row(second)).astype(BF16)

    def pair_copy(h):
        return pltpu.make_async_remote_copy(
            src_ref=part.at[h, others], dst_ref=pair.at[h],
            send_sem=pair_send.at[h], recv_sem=pair_recv.at[h],
            device_id={"tensor": twin}, device_id_type=MESH,
        )

    def reduce_send(h, k):
        c = there(k)
        return pltpu.make_async_remote_copy(
            src_ref=half.at[h, block(c)], dst_ref=landed.at[h, block(chip)],
            send_sem=rs_send.at[h, k], recv_sem=rs_recv.at[h, chip],
            device_id=device(c), device_id_type=MESH,
        )

    def reduce_arrival(h, k):
        c = there(k)
        return pltpu.make_async_remote_copy(
            src_ref=landed.at[h, block(c)], dst_ref=landed.at[h, block(c)],
            send_sem=rs_send.at[h, k], recv_sem=rs_recv.at[h, c],
            device_id=device(c), device_id_type=MESH,
        )

    def pass_on(h):
        pair_copy(h).wait_recv()
        both = part[h, mine, :].astype(F32) + pair[h].astype(F32)
        half[h] = both.astype(BF16)

        @pl.loop(1, chips)
        def _(k):
            reduce_send(h, k).start()

    for h in range(PIECES):
        @pl.loop(0, FOLD)
        def _(c):
            here = pl.ds(pl.multiple_of(c * width + h * step, step), step)
            total = lax.dot_general(
                gd_out[...], gw[here, :], (((1,), (1,)), ((), ())), preferred_element_type=F32
            ) + lax.dot_general(
                ud_out[...], uw[here, :], (((1,), (1,)), ((), ())), preferred_element_type=F32
            )
            stack[pl.ds(pl.multiple_of(c * tokens, tokens), tokens), :] = total.astype(BF16)

        part[h] = jnp.dot(back, stack[...], preferred_element_type=F32).astype(BF16)
        pair_copy(h).start()
        if h:
            pass_on(h - 1)

    pass_on(PIECES - 1)
    swap(inp_g, 1, others).wait_recv()
    unfold(inp_g, inp_out)

    for h in range(PIECES):
        @pl.loop(1, chips)
        def _(k):
            reduce_arrival(h, k).wait_recv()

        def add(k, total):
            return total + landed[h, block(there(k)), :].astype(F32)

        total = lax.fori_loop(1, chips, add, half[h, block(chip), :].astype(F32))
        fold[:, h * step:(h + 1) * step] = total

    for c in range(FOLD):
        ig_out[:, c * width:(c + 1) * width] = fold[c * local:(c + 1) * local, :].astype(BF16)

    @pl.loop(1, chips)
    def _(k):
        send(cot_g, cot_send, cot_recv, k).wait_send()
        send(inp_g, inp_send, inp_recv, k).wait_send()
        for h in range(PIECES):
            reduce_send(h, k).wait_send()

    swap(cot_g, 0, mine).wait_send()
    swap(inp_g, 1, mine).wait_send()
    for h in range(PIECES):
        pair_copy(h).wait_send()


def grads_kernel(tokens, cot_ref, inp_ref, hidden_ref, gd_ref, ud_ref, owned_ref,
                 gg_out, ug_out, dg_out, fac_out):
    dims = (((0,), (0,)), ((), ()))
    x = inp_ref[...]
    y = cot_ref[...]
    gg_out[...] = lax.dot_general(x, gd_ref[...], dims, preferred_element_type=F32).astype(BF16)
    ug_out[...] = lax.dot_general(x, ud_ref[...], dims, preferred_element_type=F32).astype(BF16)
    dg_out[...] = lax.dot_general(hidden_ref[...], y, dims, preferred_element_type=F32).astype(BF16)
    gram = lax.dot_general(owned_ref[...], y, dims, preferred_element_type=F32)
    if tokens & (tokens - 1) == 0:
        gram = gram * (1.0 / tokens)
    else:
        gram = gram / tokens
    fac_out[...] = gram.astype(BF16)


def per_device(n, layer_input, cotangent, gate_values, up_values, gate_weight, up_weight, down_weight):
    local, d = cotangent.shape
    tokens, ff = gate_values.shape
    width = d // FOLD
    blk = local * FOLD
    step = width // PIECES
    own = d // n
    inside = own % 128 == 0
    vmem = pl.BlockSpec(memory_space=pltpu.VMEM)
    hbm = pl.BlockSpec(memory_space=pl.ANY)
    shape = jax.ShapeDtypeStruct
    outs = [
        shape((tokens, d), BF16), shape((tokens, d), BF16),
        shape((tokens, ff), BF16), shape((tokens, ff), BF16), shape((tokens, ff), BF16),
        shape((tokens, own), BF16), shape((local, d), BF16),
    ]
    body = functools.partial(exchange_kernel, n)
    if not inside:
        del outs[5]

        def body(*refs):
            return exchange_kernel(n, *refs[:12], None, *refs[12:])

    gathered = pltpu.VMEM((tokens * FOLD, width), BF16)
    results = pl.pallas_call(
        body,
        out_shape=outs,
        in_specs=[vmem] * 4 + [hbm] * 3,
        out_specs=[vmem] * len(outs),
        scratch_shapes=[
            gathered, gathered,
            pltpu.VMEM((d, ff), BF16), pltpu.VMEM((d, ff), BF16), pltpu.VMEM((ff, d), BF16),
            pltpu.VMEM((tokens, ff), F32),
            pltpu.VMEM((blk, width), F32),
            pltpu.VMEM((tokens * FOLD, step), BF16),
            pltpu.VMEM((PIECES, tokens * FOLD, step), BF16),
        ] + [pltpu.VMEM((PIECES, tokens * FOLD // 2, step), BF16)] * 3
        + [pltpu.SemaphoreType.DMA((3,))]
        + [pltpu.SemaphoreType.DMA((n // 2,))] * 4
        + [pltpu.SemaphoreType.DMA((2,))] * 2
        + [pltpu.SemaphoreType.DMA((PIECES,))] * 2
        + [pltpu.SemaphoreType.DMA((PIECES, n // 2))] * 2,
        compiler_params=pltpu.CompilerParams(
            collective_id=0, has_side_effects=True, vmem_limit_bytes=60 * 2**20
        ),
        cost_estimate=pl.CostEstimate(
            flops=6 * tokens * d * ff, bytes_accessed=6 * d * ff, transcendentals=tokens * ff
        ),
        name="exchange",
    )(
        cotangent, layer_input, gate_values, up_values, gate_weight, up_weight, down_weight,
    )
    cot, inp, hidden, gd, ud = results[:5]
    if inside:
        owned = results[5]
    else:
        owned = lax.dynamic_slice_in_dim(cot, lax.axis_index("tensor") * own, own, 1)
    input_grad = results[-1]

    tile = d // 16
    whole = lambda a: pl.BlockSpec(a.shape, lambda i: (0, 0))
    gate_grad, up_grad, down_grad, factor = pl.pallas_call(
        functools.partial(grads_kernel, tokens),
        grid=(d // tile,),
        out_shape=[
            shape((d, ff), BF16), shape((d, ff), BF16), shape((ff, d), BF16), shape((own, d), BF16),
        ],
        in_specs=[
            pl.BlockSpec((tokens, tile), lambda i: (0, i)),
            pl.BlockSpec((tokens, tile), lambda i: (0, i)),
            whole(hidden), whole(gd), whole(ud), whole(owned),
        ],
        out_specs=[
            pl.BlockSpec((tile, ff), lambda i: (i, 0)),
            pl.BlockSpec((tile, ff), lambda i: (i, 0)),
            pl.BlockSpec((ff, tile), lambda i: (0, i)),
            pl.BlockSpec((own, tile), lambda i: (0, i)),
        ],
        compiler_params=pltpu.CompilerParams(vmem_limit_bytes=60 * 2**20),
        cost_estimate=pl.CostEstimate(
            flops=6 * tokens * d * ff + 2 * tokens * d * own,
            bytes_accessed=6 * d * ff + 2 * d * own, transcendentals=0,
        ),
        name="grads",
    )(cot, inp, hidden, gd, ud, owned)
    return (input_grad, gate_grad, up_grad, down_grad, factor)


def solution(mesh):
    return jax.shard_map(
        functools.partial(per_device, mesh.shape["tensor"]),
        mesh=mesh,
        in_specs=(
            P(("groups", "tensor"), None),
            P(("groups", "tensor"), None),
            P("groups", "tensor"),
            P("groups", "tensor"),
            P("groups", "tensor"),
            P("groups", "tensor"),
            P(("groups", "tensor"), None),
        ),
        out_specs=(
            P(("groups", "tensor"), None),
            P("groups", "tensor"),
            P("groups", "tensor"),
            P(("groups", "tensor"), None),
            P(("groups", "tensor"), None),
        ),
        check_vma=False,
    )
```

time: 77.3 us -> 64.7 us (0.84)
  the two profiles are of different devices: /device:TPU:31 before, /device:TPU:0 now
where the time goes in v2:
time: 64.7 us; the launch traced here: 64.4 us
  Pallas kernels  62.4 us (96%)
  local copies, waits for them, and re-layouts  1.4 us (2%)
    pallas_call x1, Pallas kernels, per_device(): pl.pallas_call(body, out_shape=outs, in_specs=[vmem] * 4 + [hbm] * 3, out...  42 us
    pallas_call x1, Pallas kernels, per_device(): pl.pallas_call(functools.partial(grads_kernel, tokens), grid=(d // tile,)...  20.4 us
    unnamed x1, local copies, waits for them, and re-layouts  1.4 us

profile of v2, /device:TPU:0, one launch (start us, length us, event | category | flops | bytes accessed | tf_op | source)
XLA Modules:
  0.0 64.4 jit_solution(8979990304098797785)
XLA Ops:
  0.6 42.0 %exchange.1 = (bf16[32,8192]{1,0:T(8,128)(2,1)}, bf16[32,8192]{1,0:T(8,128)(2,1)}, bf16[32,896]{1,0:T(8,128)(2,1)}, bf16[32,896]{1,0:T(8,128)(2,1)}, bf16[32,896...) custom-call(bf16[2,8192]{1,0:T(2,128)(2,1)} %cot_ref.1, bf16[2,8192]{1,0:T(2,128)(2,1)} %inp_ref.1, ...), custom_call_target="tpu_custom_call" | custom-call | flops 1409286144 | bytes 44040192 | tf_op jit(solution)/shard_map/exchange/pallas_call | solution.py:282
  42.7 20.4 %grads.1 = (bf16[8192,896]{1,0:T(8,128)(2,1)}, bf16[8192,896]{1,0:T(8,128)(2,1)}, bf16[896,8192]{1,0:T(8,128)(2,1)}, bf16[512,8192]{1,0:T(8,128)(2,1)}) custom-call(bf16[32,8192]{1,0:T(8,128)(2,1)} %get-tuple-element.17.cot_ref, bf16[32,8192]{1,0:T(8,128)(2,1)} %get-tuple-element.18.inp_ref, bf16[32,896]{1,0:T(8,128)(2,1)} %get-tuple-element.19.hidden_ref, ...), custom_call_target="tpu_custom_call" | custom-call | flops 1677721600 | bytes 52428800 | tf_op jit(solution)/shard_map/grads/pallas_call | solution.py:319
  63.0 1.4 %copy.13 = bf16[2,8192]{1,0:T(2,128)(2,1)} copy(bf16[2,8192]{1,0:T(2,128)(2,1)} %get-tuple-element.32) | data formatting | bytes 65536

commit v3 on v2

--- a/solution.py
+++ b/solution.py
@@ -151,11 +151,6 @@
     gd_out[...] = (hg * up * sigma * (1.0 + gate * (1.0 - sigma))).astype(BF16)
     ud_out[...] = (hg * act).astype(BF16)
 
-    @pl.loop(1, chips)
-    def _(k):
-        arrival(inp_g, inp_send, inp_recv, k).wait_recv()
-
-    swap(inp_g, 1, mine).start()
     gw_copy.wait()
     uw_copy.wait()
     back = (first == gathered_row(second)).astype(BF16)
@@ -209,6 +204,12 @@
             pass_on(h - 1)
 
     pass_on(PIECES - 1)
+
+    @pl.loop(1, chips)
+    def _(k):
+        arrival(inp_g, inp_send, inp_recv, k).wait_recv()
+
+    swap(inp_g, 1, mine).start()
     swap(inp_g, 1, others).wait_recv()
     unfold(inp_g, inp_out)
 
@@ -314,7 +315,7 @@
         owned = lax.dynamic_slice_in_dim(cot, lax.axis_index("tensor") * own, own, 1)
     input_grad = results[-1]
 
-    tile = d // 16
+    tile = d // 8
     whole = lambda a: pl.BlockSpec(a.shape, lambda i: (0, 0))
     gate_grad, up_grad, down_grad, factor = pl.pallas_call(
         functools.partial(grads_kernel, tokens),

time: 64.7 us -> 62.9 us (0.972)
  Pallas kernels: 62.4 us -> 60.6 us
    pallas_call x1, Pallas kernels: 20.4 us -> 18.6 us  [per_device(): pl.pallas_call(functools.partial(grads_kernel, tokens), grid=(d // tile,)...]
where the time goes in v3:
time: 62.9 us; the launch traced here: 62.6 us
  Pallas kernels  60.6 us (96%)
  local copies, waits for them, and re-layouts  1.4 us (2%)
  between operations  0.64 us (1%)
    pallas_call x1, Pallas kernels, per_device(): pl.pallas_call(body, out_shape=outs, in_specs=[vmem] * 4 + [hbm] * 3, out...  42 us
    pallas_call x1, Pallas kernels, per_device(): pl.pallas_call(functools.partial(grads_kernel, tokens), grid=(d // tile,)...  18.6 us
    unnamed x1, local copies, waits for them, and re-layouts  1.4 us

profile of v3, /device:TPU:0, one launch (start us, length us, event | category | flops | bytes accessed | tf_op | source)
XLA Modules:
  0.0 62.6 jit_solution(7875141317156387494)
XLA Ops:
  0.6 42.0 %exchange.1 = (bf16[32,8192]{1,0:T(8,128)(2,1)}, bf16[32,8192]{1,0:T(8,128)(2,1)}, bf16[32,896]{1,0:T(8,128)(2,1)}, bf16[32,896]{1,0:T(8,128)(2,1)}, bf16[32,896...) custom-call(bf16[2,8192]{1,0:T(2,128)(2,1)} %cot_ref.1, bf16[2,8192]{1,0:T(2,128)(2,1)} %inp_ref.1, ...), custom_call_target="tpu_custom_call" | custom-call | flops 1409286144 | bytes 44040192 | tf_op jit(solution)/shard_map/exchange/pallas_call | solution.py:283
  42.6 18.6 %grads.1 = (bf16[8192,896]{1,0:T(8,128)(2,1)}, bf16[8192,896]{1,0:T(8,128)(2,1)}, bf16[896,8192]{1,0:T(8,128)(2,1)}, bf16[512,8192]{1,0:T(8,128)(2,1)}) custom-call(bf16[32,8192]{1,0:T(8,128)(2,1)} %get-tuple-element.17.cot_ref, bf16[32,8192]{1,0:T(8,128)(2,1)} %get-tuple-element.18.inp_ref, bf16[32,896]{1,0:T(8,128)(2,1)} %get-tuple-element.19.hidden_ref, ...), custom_call_target="tpu_custom_call" | custom-call | flops 1677721600 | bytes 52428800 | tf_op jit(solution)/shard_map/grads/pallas_call | solution.py:320
  61.2 1.4 %copy.13 = bf16[2,8192]{1,0:T(2,128)(2,1)} copy(bf16[2,8192]{1,0:T(2,128)(2,1)} %get-tuple-element.32) | data formatting | bytes 65536
